TPU v7x, 1024 devices: a whole 8x8x8 slice. The times are simulated.
1024 devices in a mesh: seg: 16 (over x, core), blk: 64 (over z, y).
Axes of the slice: x: 8, y: 8, z: 8, core: 2. Of those that a mesh axis runs over, the one named last changes fastest.
Arguments:
- vel_forward: float32 [81, 524288], P(None, ('seg', 'blk')), may hold values from -0.4 to 0.4
- vel_increment: float32 [81, 524288], P(None, ('seg', 'blk')), may hold values from -0.4 to 0.4
- vel_adjoint: float32 [81, 524288], P(None, ('seg', 'blk')), may hold values from -0.4 to 0.4
- vel_incr_adjoint: float32 [81, 524288], P(None, ('seg', 'blk')), may hold values from -0.4 to 0.4
- pressure_incr: float32 [4, 524288], P(None, ('seg', 'blk')), may hold values from -1.6 to 1.6
- visc_factor: float32 [27, 524288], P(None, ('seg', 'blk')), may hold values from 0.3 to 3
- octant_scale: float32 [524288], P(('seg', 'blk')), may hold values from 1 to 4
- log_visc: float32 [32768], P('blk'), may hold values from -3 to 3
- visc_direction: float32 [32768], P('blk'), may hold values from -6 to 6
- adjacency: int32 [6, 524288], P(None, ('seg', 'blk')), may hold values from -64 to 64, as said below
- hanging: int32 [6, 524288], P(None, ('seg', 'blk')), may hold values 0 or 1
- owner_map: int32 [524288], P(('seg', 'blk')), may hold values from 0 to 32767
Outputs:
- residual: float32 [81, 524288], P(None, ('seg', 'blk'))
- hessian: float32 [32768], P('blk')
Inputs may be any that keep to these rules, and one draw needn't show every extreme that they name: `adjacency`: every nonzero entry points to an octant inside the window; some neighbours lie exactly 64 positions ahead and some exactly 64 behind; the boundary mark 0 occurs.
All inputs are finite; a program needn't handle non-finite values. No bound on the sum of `hanging` on one device may be relied on, other than what follows from the above.
Results may differ from a plain program's by a relative error of at most 0.0003.
Values sent between devices are 32-bit elements; how exact they have to be, the bound alone decides.
A program may use at most 32 MiB of HBM per device.

v0:
```python
import jax
import jax.numpy as jnp
import numpy as np
from jax import lax
from jax.sharding import PartitionSpec as P

HALO = 64


HIGH = lax.Precision.HIGHEST
BETA_REG = 1.0


def with_halo(block, sides, width):
    for axis, dim in sides:
        count = lax.axis_size(axis)
        forward = [(i, i + 1) for i in range(count - 1)]
        backward = [(target, source) for source, target in forward]
        low = lax.ppermute(
            lax.slice_in_dim(block, block.shape[dim] - width, None, axis=dim), axis, forward
        )
        high = lax.ppermute(lax.slice_in_dim(block, 0, width, axis=dim), axis, backward)
        block = jnp.concatenate([low, block, high], axis=dim)
    return block


def element_tables():
    gauss = np.array([-np.sqrt(0.6), 0.0, np.sqrt(0.6)])
    weights_one = np.array([5.0 / 9.0, 8.0 / 9.0, 5.0 / 9.0])
    values = np.stack(
        [gauss * (gauss - 1.0) / 2.0, 1.0 - gauss * gauss, gauss * (gauss + 1.0) / 2.0]
    )
    slopes = np.stack([gauss - 0.5, -2.0 * gauss, gauss + 0.5])
    gradient = np.zeros((3, 27, 27))
    quad_weight = np.zeros(27)
    coords = np.zeros((27, 3))
    for first in range(3):
        for second in range(3):
            for third in range(3):
                point = (first * 3 + second) * 3 + third
                quad_weight[point] = weights_one[first] * weights_one[second] * weights_one[third]
                coords[point] = [gauss[first], gauss[second], gauss[third]]
                for node_a in range(3):
                    for node_b in range(3):
                        for node_c in range(3):
                            node = (node_a * 3 + node_b) * 3 + node_c
                            gradient[0, point, node] = (
                                slopes[node_a, first]
                                * values[node_b, second]
                                * values[node_c, third]
                            )
                            gradient[1, point, node] = (
                                values[node_a, first]
                                * slopes[node_b, second]
                                * values[node_c, third]
                            )
                            gradient[2, point, node] = (
                                values[node_a, first]
                                * values[node_b, second]
                                * slopes[node_c, third]
                            )
    pairs = [(0, 0), (1, 1), (2, 2), (0, 1), (1, 2), (0, 2)]
    strain = np.zeros((162, 81))
    for comp in range(6):
        left, right = pairs[comp]
        strain[comp * 27 : (comp + 1) * 27, left * 27 : (left + 1) * 27] += 0.5 * gradient[right]
        strain[comp * 27 : (comp + 1) * 27, right * 27 : (right + 1) * 27] += 0.5 * gradient[left]
    diverge = strain[0:27] + strain[27:54] + strain[54:81]
    contract = np.repeat(np.array([1.0, 1.0, 1.0, 2.0, 2.0, 2.0]), 27)
    basis_press = np.concatenate([np.ones((27, 1)), coords], 1)
    select = np.zeros((81, 162))
    for face in range(6):
        direction = face // 2
        side = 2 * (face % 2)
        nodes = [
            node for node in range(27) if (node // 9, node // 3 % 3, node % 3)[direction] == side
        ]
        for comp in range(3):
            for place in range(9):
                select[comp * 27 + nodes[place], face * 27 + comp * 9 + place] = 1.0
    return (
        jnp.asarray(strain, jnp.float32),
        jnp.asarray(diverge, jnp.float32),
        jnp.asarray(basis_press, jnp.float32),
        jnp.asarray(quad_weight, jnp.float32),
        jnp.asarray(contract, jnp.float32),
        jnp.asarray(select, jnp.float32),
    )


def element_work(tables, velocity, pressure, factors, scale, log_oct, dir_oct):
    strain, diverge, basis_press, quad_weight, contract, select = tables
    rates = jnp.einsum("sv,kvn->ksn", strain, velocity, precision=HIGH) * scale[None, None, :]
    rate_fwd, rate_inc, rate_adj, rate_incadj = (rates[0], rates[1], rates[2], rates[3])
    jacobian = 1.0 / (scale * scale * scale)
    weighted = quad_weight[:, None] * jacobian[None, :]
    viscosity = jnp.exp(log_oct)[None, :] * factors
    coef = jnp.tile(2.0 * viscosity * weighted, (6, 1)) * contract[:, None]
    stress = coef * (rate_incadj + dir_oct[None, :] * rate_adj)
    press_quad = weighted * jnp.dot(basis_press, pressure, precision=HIGH)
    local = scale[None, :] * (
        jnp.dot(strain.T, stress, precision=HIGH) - jnp.dot(diverge.T, press_quad, precision=HIGH)
    )
    contrib = coef * (
        rate_inc * rate_adj + rate_fwd * rate_incadj + dir_oct[None, :] * rate_fwd * rate_adj
    )
    grad = jnp.sum(contrib, axis=0)
    face = jnp.dot(select.T, local, precision=HIGH)
    return (local, face, grad)


def assemble(tables, faces3, columns, valid, hanging):
    select = tables[5]
    width = faces3.shape[2]
    pieces = []
    for face in range(6):
        other = face ^ 1
        picked = jnp.take(faces3[other], jnp.clip(columns[face], 0, width - 1), axis=1)
        weight = jnp.where(valid[face], jnp.where(hanging[face] == 1, 0.25, 1.0), 0.0).astype(
            picked.dtype
        )
        pieces.append(picked * weight[None, :])
    return jnp.dot(select, jnp.concatenate(pieces, 0), precision=HIGH)


def laplace(field):
    padded = jnp.pad(field, 1)
    return 2.0 * field - padded[:-2] - padded[2:]


def per_device(
    vel_forward,
    vel_increment,
    vel_adjoint,
    vel_incr_adjoint,
    pressure_incr,
    visc_factor,
    octant_scale,
    log_visc,
    visc_direction,
    adjacency,
    hanging,
    owner_map,
):
    tables = element_tables()
    owned = log_visc.shape[0]
    count = vel_forward.shape[1]
    full_log, full_dir = (
        lax.all_gather(log_visc, "blk", axis=0, tiled=True),
        lax.all_gather(visc_direction, "blk", axis=0, tiled=True),
    )
    log_oct = jnp.take(full_log, owner_map)
    dir_oct = jnp.take(full_dir, owner_map)
    velocity = jnp.stack([vel_forward, vel_increment, vel_adjoint, vel_incr_adjoint])
    local, face, grad = element_work(
        tables, velocity, pressure_incr, visc_factor, octant_scale, log_oct, dir_oct
    )
    padded = with_halo(face, ((("seg", "blk"), 1),), HALO)
    positions = jnp.arange(count, dtype=jnp.int32)
    columns = positions[None, :] + adjacency + HALO
    residual = local + assemble(
        tables, padded.reshape(6, 27, padded.shape[1]), columns, adjacency != 0, hanging
    )
    partial_sum = jax.ops.segment_sum(grad, owner_map, num_segments=owned * lax.axis_size("blk"))
    owner_index = lax.axis_index("blk") * owned
    totals = lax.psum(partial_sum, ("seg", "blk"))
    summed = lax.dynamic_slice_in_dim(totals, owner_index, owned, 0)
    smoothing = lax.dynamic_slice_in_dim(laplace(full_dir), owner_index, owned, 0)
    hessian = summed + BETA_REG * smoothing
    return (residual, hessian)


def solution(mesh):
    placed = (
        P(None, ("seg", "blk")),
        P(None, ("seg", "blk")),
        P(None, ("seg", "blk")),
        P(None, ("seg", "blk")),
        P(None, ("seg", "blk")),
        P(None, ("seg", "blk")),
        P(("seg", "blk")),
        P("blk"),
        P("blk"),
        P(None, ("seg", "blk")),
        P(None, ("seg", "blk")),
        P(("seg", "blk")),
    )
    return jax.shard_map(
        per_device,
        mesh=mesh,
        in_specs=placed,
        out_specs=(P(None, ("seg", "blk")), P("blk")),
        check_vma=False,
    )
```

profile of v0, /device:TPU:1, one launch (start us, length us, event | category | flops | bytes accessed | tf_op | source)
XLA Modules:
  0.0 412.8 jit_solution(14255046551272012950)
XLA Ops:
  7.2 0.7 compare_select_fusion.12
  7.9 51.8 %all-gather = f32[64,1,512]{2,1,0:T(1,128)S(1)} all-gather(f32[1,1,512]{2,1,0:T(1,128)} %bitcast.95), channel_id=1, replica_groups=mesh['seg'=16,'blk'=64] {'blk'}, dimensions={0}, use_global_device_ids=true | all-gather | bytes 133120 | tf_op jit(solution)/shard_map/all_gather | solution.py:149
  59.7 35.3 %all-gather.1 = f32[64,1,512]{2,1,0:T(1,128)S(1)} all-gather(f32[1,1,512]{2,1,0:T(1,128)} %bitcast.96), channel_id=1, replica_groups=mesh['seg'=16,'blk'=64] {'blk'}, dimensions={0}, use_global_device_ids=true | all-gather | bytes 133120 | tf_op jit(solution)/shard_map/all_gather | solution.py:150
  95.1 3.1 gather_fusion
  98.3 3.1 gather_fusion.1
  101.8 1.3 fusion
  103.3 3.9 scatter_custom_fusion
  109.0 2.7 collective-permute-start
  111.6 28.8 %collective-permute-start.1 = (f32[162,64]{1,0:T(8,128)S(1)}, f32[162,64]{1,0:T(8,128)S(1)}, u32[]{:S(2)}, u32[]{:S(2)}) collective-permute-start(f32[162,64]{1,0:T(8,128)S(1)} %get-tuple-element.11), channel_id=1, source_target_pairs={{1,0},{2,1},{3,2},{4,3},{5,4},{6,5},{7,6},{8,7},{9,8},{10,9},{11,1... | collective-permute-start | bytes 124424 | tf_op jit(solution)/shard_map/ppermute | solution.py:22
  140.9 1.0 collective-permute-done.1
  143.3 1.0 gather_fusion.7
  144.3 1.0 gather_fusion.6
  145.4 1.0 gather_fusion.5
  146.4 1.0 gather_fusion.4
  147.5 1.0 gather_fusion.3
  148.5 1.0 gather_fusion.2
  149.6 0.6 fusion.22
  150.2 0.6 convolution_add_fusion.4
  150.8 0.6 convolution_add_fusion.3
  151.4 0.6 convolution_add_fusion.2
  152.0 0.6 convolution_add_fusion.1
  152.5 1.2 fusion.3
  153.8 250.9 %all-reduce.3.cloned.1.call-done = f32[32768]{0:T(1024)} async-done(((f32[32768]{0:T(1024)}), f32[32768]{0:T(1024)}) %all-reduce.3.cloned.1.call-update) | async-done | bytes 131088 | tf_op jit(solution)/shard_map/psum | solution.py:166
  404.6 1.3 fusion.52
  (92 shorter events, 3.7 us)
Async XLA Ops:
  7.2 100.1 %copy-start = (f32[4,512]{1,0:T(4,128)S(1)}, f32[4,512]{1,0:T(4,128)}, u32[]{:S(2)}) copy-start(f32[4,512]{1,0:T(4,128)} %param.26) | copy-start | bytes 24580
  7.2 397.5 %all-reduce.3.cloned.1.call-start = ((), (), s32[]{:S(2)}) async-start(), calls=%async_computation | async-start | bytes 262144 | tf_op jit(solution)/shard_map/psum | solution.py:166
  98.2 3.3 copy-start.16
  98.2 3.3 copy-start.20
  98.2 3.3 copy-start.9
  98.2 3.3 copy-start.22
  98.2 3.5 copy-start.1
  98.3 3.5 copy-start.2
  98.3 3.5 copy-start.3
  98.3 3.5 copy-start.4
  98.3 3.4 copy-start.6
  103.1 4.2 %copy-start.18 = (f32[27,4]{1,0:T(8,128)S(1)}, f32[27,4]{1,0:T(8,128)}, u32[]{:S(2)}) copy-start(f32[27,4]{1,0:T(8,128)} %constant.19.clone) | copy-start | bytes 1300
  103.1 4.4 %copy-start.17 = (f32[27,81]{1,0:T(8,128)S(1)}, f32[27,81]{1,0:T(8,128)}, u32[]{:S(2)}) copy-start(f32[27,81]{1,0:T(8,128)} %constant.18.clone) | copy-start | bytes 26248
  103.1 4.7 %copy-start.7 = (f32[162,81]{1,0:T(8,128)S(1)}, f32[162,81]{1,0:T(8,128)}, u32[]{:S(2)}) copy-start(f32[162,81]{1,0:T(8,128)} %constant.17.clone) | copy-start | bytes 157468
  103.3 5.1 %copy-start.5 = (f32[81,162]{1,0:T(8,128)S(1)}, f32[81,162]{1,0:T(8,128)}, u32[]{:S(2)}) copy-start(f32[81,162]{1,0:T(8,128)} %constant.22.clone) | copy-start | bytes 157468
  107.3 33.2 %copy-start.8 = (s32[6,512]{1,0:T(8,128)S(1)}, s32[6,512]{1,0:T(8,128)}, u32[]{:S(2)}) copy-start(s32[6,512]{1,0:T(8,128)} %param.31) | copy-start | bytes 36868
  107.9 33.0 %copy-start.19 = (s32[6,512]{1,0:T(8,128)S(1)}, s32[6,512]{1,0:T(8,128)}, u32[]{:S(2)}) copy-start(s32[6,512]{1,0:T(8,128)} %param.32) | copy-start | bytes 36868
  109.0 32.0 %collective-permute-start = (f32[162,64]{1,0:T(8,128)S(1)}, f32[162,64]{1,0:T(8,128)S(1)}, u32[]{:S(2)}, u32[]{:S(2)}) collective-permute-start(f32[162,64]{1,0:T(8,128)S(1)} %get-tuple-element.10), channel_id=1, source_target_pairs={{0,1},{1,2},{2,3},{3,4},{4,5},{5,6},{6,7},{7,8},{8,9},{9,10},{10,1... | collective-permute-start | bytes 124424 | tf_op jit(solution)/shard_map/ppermute | solution.py:19
  111.6 30.3 %collective-permute-start.1 = (f32[162,64]{1,0:T(8,128)S(1)}, f32[162,64]{1,0:T(8,128)S(1)}, u32[]{:S(2)}, u32[]{:S(2)}) collective-permute-start(f32[162,64]{1,0:T(8,128)S(1)} %get-tuple-element.11), channel_id=1, source_target_pairs={{1,0},{2,1},{3,2},{4,3},{5,4},{6,5},{7,6},{8,7},{9,8},{10,9},{11,1... | collective-permute-start | bytes 124424 | tf_op jit(solution)/shard_map/ppermute | solution.py:22
  144.3 5.3 %copy-start.15 = (f32[81,27]{1,0:T(8,128)S(1)}, f32[81,27]{1,0:T(8,128)}, u32[]{:S(2)}) copy-start(f32[81,27]{1,0:T(8,128)} %constant.79) | copy-start | bytes 26248
  145.4 4.8 %copy-start.14 = (f32[81,27]{1,0:T(8,128)S(1)}, f32[81,27]{1,0:T(8,128)}, u32[]{:S(2)}) copy-start(f32[81,27]{1,0:T(8,128)} %constant.80) | copy-start | bytes 26248
  146.4 4.3 %copy-start.13 = (f32[81,27]{1,0:T(8,128)S(1)}, f32[81,27]{1,0:T(8,128)}, u32[]{:S(2)}) copy-start(f32[81,27]{1,0:T(8,128)} %constant.81) | copy-start | bytes 26248
  147.5 3.9 copy-start.12
  149.6 2.4 copy-start.11
  (2 other events, 3.8 us)
Sparse Core Ops, SparseCore 0:
  107.3 297.2 all-reduce.2
where the time goes:
time: 413 us
  waiting for transfers between devices  252 us (61%)
  blocking collectives  87.1 us (21%)
  starting transfers between devices  31.5 us (8%)
  between operations  14.8 us (4%)
  local copies, waits for them, and re-layouts  14.1 us (3%)
  matrix products  6.96 us (2%)
  other arithmetic  6.51 us (2%)
    psum x1, waiting for transfers between devices, per_device(): totals = lax.psum(partial_sum, ('seg', 'blk'))  251 us
    all_gather x1, blocking collectives, per_device(): lax.all_gather(log_visc, 'blk', axis=0, tiled=True)  51.8 us
    all_gather x1, blocking collectives, per_device(): lax.all_gather(visc_direction, 'blk', axis=0, tiled=True)  35.3 us
    ppermute x1, starting transfers between devices, with_halo(): lax.ppermute(lax.slice_in_dim(block, 0, width, axis=dim), axis, backward)  28.8 us
  transfers between devices with their start and end apart: 3, of which 2 were waited for; matrix products, arithmetic and copies ran while one was open for 3% of the time, Pallas kernels for 0%

commit v1 on v0

v1 whole, which is shorter than its diff:
```python
import functools

import jax
import jax.numpy as jnp
import ml_dtypes
import numpy as np
from jax import lax
from jax.experimental import pallas as pl
from jax.experimental.pallas import tpu as pltpu
from jax.sharding import PartitionSpec as P

MESH = pl.DeviceIdType.MESH
F32 = jnp.float32
BF16 = jnp.bfloat16
BETA_REG = 1.0
SHEAR = (1.0, 1.0, 1.0, 2.0, 2.0, 2.0)


def element_tables():
    gauss = np.array([-np.sqrt(0.6), 0.0, np.sqrt(0.6)])
    weights_one = np.array([5.0 / 9.0, 8.0 / 9.0, 5.0 / 9.0])
    values = np.stack([gauss * (gauss - 1.0) / 2.0, 1.0 - gauss * gauss, gauss * (gauss + 1.0) / 2.0])
    slopes = np.stack([gauss - 0.5, -2.0 * gauss, gauss + 0.5])
    gradient = np.zeros((3, 27, 27))
    for r in range(3):
        parts = [slopes if d == r else values for d in range(3)]
        gradient[r] = np.einsum("ia,jb,kc->abcijk", *parts).reshape(27, 27)
    quad_weight = np.einsum("a,b,c->abc", weights_one, weights_one, weights_one).reshape(27)
    coords = np.stack([g.reshape(27) for g in np.meshgrid(gauss, gauss, gauss, indexing="ij")], 1)
    pairs = [(0, 0), (1, 1), (2, 2), (0, 1), (1, 2), (0, 2)]
    strain = np.zeros((6, 27, 81))
    for comp, (left, right) in enumerate(pairs):
        strain[comp, :, left * 27 : (left + 1) * 27] += 0.5 * gradient[right]
        strain[comp, :, right * 27 : (right + 1) * 27] += 0.5 * gradient[left]
    select = np.zeros((81, 6, 32))
    for face in range(6):
        direction, side = face // 2, 2 * (face % 2)
        nodes = [n for n in range(27) if (n // 9, n // 3 % 3, n % 3)[direction] == side]
        for comp in range(3):
            for place in range(9):
                select[comp * 27 + nodes[place], face, comp * 9 + place] = 1.0
    return strain.astype(np.float32), quad_weight, coords, select


def halves(table):
    high = table.astype(ml_dtypes.bfloat16)
    low = (table - high.astype(np.float32)).astype(ml_dtypes.bfloat16)
    return high, low


def constants():
    strain, quad_weight, coords, select = element_tables()
    padded = np.zeros((6, 32, 81), np.float32)
    padded[:, :27] = strain
    padded = padded.reshape(192, 81)
    high, low = halves(padded)
    rate = np.zeros((192, 256), ml_dtypes.bfloat16)
    rate[:, 0:80], rate[:, 80:160], rate[:, 160:240] = high[:, :80], high[:, :80], low[:, :80]
    rate[:, 240], rate[:, 241], rate[:, 242] = high[:, 80], high[:, 80], low[:, 80]
    rows = np.zeros((288, 192), np.float32)
    rows[:81] = padded.T
    rows[88:280] = select.reshape(81, 192).T @ padded.T
    high, low = halves(rows)
    force = np.concatenate([high, high, low], 1)
    place = np.zeros((96, 384), ml_dtypes.bfloat16)
    place[:81, :192] = select.reshape(81, 192)
    place[:81, 192:] = select.reshape(81, 192)
    points = np.zeros((4, 32, 128), np.float32)
    points[0, :27] = quad_weight[:, None]
    for d in range(3):
        points[d + 1, :27] = coords[:, d, None]
    return rate, force, place, points


def split(x):
    high = x.astype(BF16)
    return high, (x - high.astype(F32)).astype(BF16)


def iota(shape, dim):
    return lax.broadcasted_iota(jnp.int32, shape, dim)


def kernel(
    nz, ny, nseg,
    vel_f, vel_i, vel_a, vel_ia, press_h, visc_h, scale_h, log_h, dir_h, adj_h, hang_h, own_h,
    rate_h, force_h, place_h, points_h,
    res_out, hess_out,
    vel, press, visc, scale, log_v, dir_v, adj, hang, own, rate, force, place, points,
    rates, vstack, keys, table, side, onehot, sums, reply, gathered, partial, faces, halo, hits,
    stress, local, spread, picked, res, hess,
    load_sem, out_sem, key_send, key_recv, tab_send, tab_recv, side_send, side_recv,
    sum_send, sum_recv, rep_send, rep_recv, par_send, par_recv, halo_send, halo_recv,
):
    seg, blk = lax.axis_index("seg"), lax.axis_index("blk")
    z, y = blk // ny, lax.rem(blk, ny)
    nblk = nz * ny
    flat = seg * nblk + blk
    total = nseg * nblk
    after, before = lax.rem(flat + 1, total), lax.rem(flat + total - 1, total)
    after, before = (after // nblk, lax.rem(after, nblk)), (before // nblk, lax.rem(before, nblk))
    z_peer = [(seg, lax.rem(z + k, nz) * ny + y) for k in range(nz)]
    y_peer = [(seg, z * ny + lax.rem(y + k, ny)) for k in range(ny)]
    s_peer = [(lax.rem(seg + k, nseg), blk) for k in range(nseg)]

    pairs = [
        (vel_f, vel.at[0]), (vel_i, vel.at[1]), (vel_a, vel.at[2]), (vel_ia, vel.at[3]), (rate_h, rate), (visc_h, visc),
        (scale_h, scale), (own_h, own), (points_h, points), (log_h, log_v), (dir_h, dir_v), (adj_h, adj), (hang_h, hang),
        (force_h, force), (press_h, press), (place_h, place),
    ]
    loads = [pltpu.make_async_copy(a, b, load_sem.at[i]) for i, (a, b) in enumerate(pairs)]
    for load in loads:
        load.start()

    barrier = pltpu.get_barrier_semaphore()
    peers = z_peer[1:] + y_peer[1:] + [after, before] + s_peer[1:]
    for peer in peers:
        pl.semaphore_signal(barrier, inc=1, device_id=peer, device_id_type=MESH)

    def send(src, dst, send_sem, recv_sem, peer):
        pltpu.make_async_remote_copy(
            src_ref=src, dst_ref=dst, send_sem=send_sem, recv_sem=recv_sem, device_id=peer, device_id_type=MESH
        ).start()

    def drain(ref, sem):
        pltpu.make_async_copy(ref, ref, sem).wait()

    for i in range(4):
        loads[i].wait()
        if i == 0:
            loads[4].wait()
        high, low = split(vel[i, 0:80, :])
        last_high = vel[i, 80:81, :].astype(BF16).astype(F32)
        last_low = vel[i, 80:81, :] - last_high
        row = iota((16, 512), 0)
        tail = jnp.where((row == 0) | (row == 2), last_high, jnp.where(row == 1, last_low, 0.0)).astype(BF16)
        vstack[0:80, :] = high
        vstack[80:160, :] = low
        vstack[160:240, :] = high
        vstack[240:256, :] = tail
        rates[i] = jnp.dot(rate[...], vstack[...], preferred_element_type=F32)

    for i in range(5, 9):
        loads[i].wait()
    inverse = 1.0 / scale[...]
    factor = jnp.concatenate([visc[...], jnp.zeros((5, 512), F32)], 0)
    base = 2.0 * factor * points[0][:, 0:1] * inverse
    first = jnp.zeros((32, 512), F32)
    second = jnp.zeros((32, 512), F32)
    for c in range(6):
        at = pl.ds(32 * c, 32)
        fwd, inc, adjoint, incadj = rates[0, at, :], rates[1, at, :], rates[2, at, :], rates[3, at, :]
        first += SHEAR[c] * (inc * adjoint + fwd * incadj)
        second += SHEAR[c] * (fwd * adjoint)
    sum_first = jnp.sum(base * first, axis=0, keepdims=True)
    sum_second = jnp.sum(base * second, axis=0, keepdims=True)
    owner = own[...]
    row_of = owner // 128
    block_of = row_of // 4
    block_y = lax.rem(block_of, ny)
    slot = lax.rem(y - block_y + ny, ny)
    key = (block_of // ny) * (4 * ny) + slot * 4 + lax.rem(row_of, 4)
    column = lax.rem(owner, 128)
    keys[0, 0:1, :] = key.astype(F32)
    keys[0, 1:2, :] = column.astype(F32)
    keys[0, 2:3, :] = sum_first
    keys[0, 3:4, :] = sum_second
    loads[9].wait()
    loads[10].wait()
    table[0, 0:4, :] = log_v[...]
    table[0, 4:8, :] = dir_v[...]

    pl.semaphore_wait(barrier, len(peers))
    for k in range(1, nz):
        send(keys.at[0], keys.at[k], key_send, key_recv, z_peer[k])
    for k in range(1, ny):
        send(table.at[0], table.at[k], tab_send, tab_recv, y_peer[k])
    send(table.at[0], side.at[0], side_send.at[0], side_recv.at[0], after)
    send(table.at[0], side.at[1], side_send.at[1], side_recv.at[1], before)

    loads[11].wait()
    loads[12].wait()
    lane = lax.rem(iota((1, 512), 1), 128)
    for f in range(6):
        reach = adj[f : f + 1, :]
        target = lax.rem(lane + reach + 384, 256)
        weight = jnp.where(reach != 0, jnp.where(hang[f : f + 1, :] == 1, 0.25, 1.0), 0.0)
        hits[f] = jnp.where(iota((256, 512), 0) == target, weight, 0.0).astype(BF16)

    drain(keys.at[pl.ds(0, nz - 1)], key_recv)
    rho = iota((8 * ny, 512), 0)
    wanted = (z * (4 * ny) + (rho // 8) * 4 + lax.rem(rho, 4)).astype(F32)
    is_second = lax.rem(rho, 8) >= 4
    acc = jnp.zeros((16 * ny, 128), F32)
    for d in range(nz):
        hit = keys[d, 0:1, :] == wanted
        value = jnp.where(is_second, keys[d, 3:4, :], keys[d, 2:3, :])
        value = jnp.where(hit, value, 0.0)
        high, low = split(value)
        onehot[d] = jnp.where(iota((128, 512), 0).astype(F32) == keys[d, 1:2, :], 1.0, 0.0).astype(BF16)
        acc += lax.dot_general(
            jnp.concatenate([high, low], 0), onehot[d], (((1,), (1,)), ((), ())), preferred_element_type=F32
        )
    dense = acc[0 : 8 * ny, :] + acc[8 * ny : 16 * ny, :]
    for k in range(ny):
        sums[0, k] = dense[8 * k : 8 * k + 8, :]
    for k in range(1, ny):
        send(sums.at[0, k], sums.at[1, k], sum_send, sum_recv, y_peer[ny - k])

    drain(table.at[pl.ds(0, ny - 1)], tab_recv)
    row = iota((8 * ny, 512), 0)
    for part in range(2):
        rows = jnp.concatenate([table[k, 4 * part : 4 * part + 4, :] for k in range(ny)], 0)
        high, low = split(rows)
        spread[part] = jnp.concatenate([high, low], 0)
    key_row = z * (4 * ny) + lax.rem(iota((8 * ny, 512), 0), 4 * ny)
    for d in range(nz):
        pick = jnp.where(keys[d, 0:1, :] == key_row.astype(F32), 1.0, 0.0).astype(BF16)
        mask = onehot[d].astype(F32)
        for part in range(2):
            found = lax.dot_general(spread[part], pick, (((0,), (0,)), ((), ())), preferred_element_type=F32)
            answer = jnp.sum(found * mask, axis=0, keepdims=True)
            reply[d, part : part + 1, :] = answer
    for d in range(1, nz):
        send(reply.at[d], gathered.at[d], rep_send, rep_recv, z_peer[nz - d])

    drain(sums.at[1, pl.ds(0, ny - 1)], sum_recv)
    mine = sums[0, 0]
    for k in range(1, ny):
        mine += sums[1, k]
    share = jnp.exp(table[0, 0:4, :]) * (mine[0:4, :] + table[0, 4:8, :] * mine[4:8, :])
    partial[seg] = share
    for k in range(1, nseg):
        send(partial.at[seg], partial.at[seg], par_send, par_recv, s_peer[k])

    drain(gathered.at[pl.ds(0, nz - 1)], rep_recv)
    found = reply[0]
    for k in range(1, nz):
        found += gathered[k]
    viscosity = jnp.exp(found[0:1, :]) * base
    direction = found[1:2, :]
    for i in range(13, 16):
        loads[i].wait()
    pressure = (
        press[0:1, :] + points[1][:, 0:1] * press[1:2, :] + points[2][:, 0:1] * press[2:3, :]
        + points[3][:, 0:1] * press[3:4, :]
    ) * points[0][:, 0:1] * (inverse * inverse)
    for c in range(6):
        at = pl.ds(32 * c, 32)
        value = SHEAR[c] * viscosity * (rates[3, at, :] + direction * rates[2, at, :])
        if c < 3:
            value -= pressure
        high, low = split(value)
        stress[32 * c : 32 * c + 32, :] = high
        stress[192 + 32 * c : 224 + 32 * c, :] = low
        stress[384 + 32 * c : 416 + 32 * c, :] = high
    local[...] = jnp.dot(force[...], stress[...], preferred_element_type=F32)
    for b in range(4):
        faces[b] = local[88:280, 128 * b : 128 * b + 128]
    send(faces.at[3], halo.at[0], halo_send.at[0], halo_recv.at[0], after)
    send(faces.at[0], halo.at[1], halo_send.at[1], halo_recv.at[1], before)

    low_lane = iota((192, 128), 1) < 64

    def window(b):
        last = halo[0] if b == 0 else faces[b - 1]
        following = halo[1] if b == 3 else faces[b + 1]
        beside_high, beside_low = split(jnp.where(low_lane, following, last))
        own_high, own_low = split(faces[b])
        for f in range(6):
            at = slice(32 * f, 32 * f + 32)
            window_rows = jnp.concatenate([
                jnp.concatenate([beside_high[at], own_high[at]], 1),
                jnp.concatenate([beside_low[at], own_low[at]], 1),
            ], 0)
            other = f ^ 1
            got = jnp.dot(window_rows, hits[other, :, 128 * b : 128 * b + 128], preferred_element_type=F32)
            picked[32 * other : 32 * other + 32, 128 * b : 128 * b + 128] = got[0:32].astype(BF16)
            picked[192 + 32 * other : 224 + 32 * other, 128 * b : 128 * b + 128] = got[32:64].astype(BF16)

    window(1)
    window(2)
    drain(halo.at[0], halo_recv.at[0])
    window(0)
    drain(halo.at[1], halo_recv.at[1])
    window(3)
    added = jnp.dot(place[...], picked[...], preferred_element_type=F32)
    res[...] = local[0:81, :] + added[0:81, :]
    out_res = pltpu.make_async_copy(res, res_out, out_sem.at[0])
    out_res.start()

    drain(side.at[0], side_recv.at[0])
    drain(side.at[1], side_recv.at[1])
    tile = table[0]
    row, lane = iota((8, 128), 0), iota((8, 128), 1)
    up = pltpu.roll(tile, 1, 1)
    up_row = pltpu.roll(up, 1, 0)
    up_side = pltpu.roll(pltpu.roll(side[0], 1, 1), 5, 0)
    up_side = jnp.where(blk == 0, 0.0, up_side)
    prev = jnp.where(lane == 0, jnp.where(row == 4, up_side, up_row), up)
    down = pltpu.roll(tile, 127, 1)
    down_row = pltpu.roll(down, 7, 0)
    down_side = pltpu.roll(pltpu.roll(side[1], 127, 1), 3, 0)
    down_side = jnp.where(blk == nblk - 1, 0.0, down_side)
    following = jnp.where(lane == 127, jnp.where(row == 7, down_side, down_row), down)
    smooth = BETA_REG * (2.0 * tile - prev - following)

    drain(partial.at[pl.ds(0, nseg - 1)], par_recv)
    result = partial[0]
    for k in range(1, nseg):
        result += partial[k]
    hess[...] = result + smooth[4:8, :]
    out_hess = pltpu.make_async_copy(hess, hess_out, out_sem.at[1])
    out_hess.start()

    drain(keys.at[pl.ds(0, nz - 1)], key_send)
    drain(table.at[pl.ds(0, ny - 1)], tab_send)
    drain(sums.at[1, pl.ds(0, ny - 1)], sum_send)
    drain(gathered.at[pl.ds(0, nz - 1)], rep_send)
    drain(partial.at[pl.ds(0, nseg - 1)], par_send)
    for i in range(2):
        drain(side.at[i], side_send.at[i])
        drain(halo.at[i], halo_send.at[i])
    out_res.wait()
    out_hess.wait()


def per_device(nz, ny, nseg, tables, *args):
    vel = args[:4]
    press, visc, scale, log_visc, direction, adj, hang, owner = args[4:]
    dma = pltpu.SemaphoreType.DMA
    vmem = pltpu.VMEM
    residual, hessian = pl.pallas_call(
        functools.partial(kernel, nz, ny, nseg),
        out_shape=(jax.ShapeDtypeStruct((81, 512), F32), jax.ShapeDtypeStruct((4, 128), F32)),
        in_specs=[pl.BlockSpec(memory_space=pl.ANY)] * 16,
        out_specs=(pl.BlockSpec(memory_space=pl.ANY),) * 2,
        scratch_shapes=[
            vmem((4, 81, 512), F32), vmem((4, 512), F32), vmem((27, 512), F32), vmem((1, 512), F32),
            vmem((4, 128), F32), vmem((4, 128), F32), vmem((6, 512), jnp.int32), vmem((6, 512), jnp.int32),
            vmem((1, 512), jnp.int32),
            vmem((192, 256), BF16), vmem((288, 576), BF16), vmem((96, 384), BF16), vmem((4, 32, 128), F32),
            vmem((4, 192, 512), F32),
            vmem((256, 512), BF16),
            vmem((nz, 4, 512), F32),
            vmem((ny, 8, 128), F32),
            vmem((2, 8, 128), F32),
            vmem((nz, 128, 512), BF16),
            vmem((2, ny, 8, 128), F32),
            vmem((nz, 2, 512), F32),
            vmem((nz, 2, 512), F32),
            vmem((nseg, 4, 128), F32),
            vmem((4, 192, 128), F32),
            vmem((2, 192, 128), F32),
            vmem((6, 256, 512), BF16),
            vmem((576, 512), BF16),
            vmem((288, 512), F32),
            vmem((2, 8 * ny, 128), BF16),
            vmem((384, 512), BF16),
            vmem((81, 512), F32), vmem((4, 128), F32),
            dma((16,)), dma((2,)), dma, dma, dma, dma, dma((2,)), dma((2,)),
            dma, dma, dma, dma, dma, dma, dma((2,)), dma((2,)),
        ],
        compiler_params=pltpu.CompilerParams(
            collective_id=0, has_side_effects=True, vmem_limit_bytes=32 * 1024 * 1024
        ),
    )(
        *vel, press, visc, scale.reshape(1, 512), log_visc.reshape(4, 128), direction.reshape(4, 128), adj, hang,
        owner.reshape(1, 512), *tables,
    )
    return residual, hessian.reshape(512)


def solution(mesh):
    nseg, nblk = mesh.shape["seg"], mesh.shape["blk"]
    ny = max(d for d in (1, 2, 4, 8) if d * d <= nblk)
    tables = constants()
    octants = P(None, ("seg", "blk"))
    line = P(("seg", "blk"))
    placed = (octants,) * 6 + (line, P("blk"), P("blk"), octants, octants, line)

    def step(*args):
        return per_device(nblk // ny, ny, nseg, [jnp.asarray(t) for t in tables], *args)

    return jax.shard_map(step, mesh=mesh, in_specs=placed, out_specs=(octants, P("blk")), check_vma=False)
```

time: 413 us -> 57.9 us (0.14)
  waiting for transfers between devices: 252 us -> 0 us
  blocking collectives: 87.1 us -> 0 us
  Pallas kernels: 0 us -> 43.7 us
  starting transfers between devices: 31.5 us -> 0 us
  between operations: 14.8 us -> 0.68 us
  matrix products: 6.96 us -> 0 us
  other arithmetic: 6.51 us -> 0 us
    psum x1 -> x0, waiting for transfers between devices: 251 us -> none  [per_device(): totals = lax.psum(partial_sum, ('seg', 'blk'))]
    all_gather x2 -> x0, blocking collectives: 87.1 us -> none  [the longest x1 51.8 us: per_device(): lax.all_gather(log_visc, 'blk', axis=0, tiled=True)]
    pallas_call x0 -> x1, Pallas kernels: none -> 43.7 us  [per_device(): pl.pallas_call(functools.partial(kernel, nz, ny, nseg), out_shape=(jax.Sh...]
    ppermute x2 -> x0, starting transfers between devices: 31.5 us -> none  [the longest x1 28.8 us: with_halo(): lax.ppermute(lax.slice_in_dim(block, 0, width, axis=dim), axis, backward)]
    unnamed x46 -> x34, local copies, waits for them, and re-layouts: 0.15 us -> 12.9 us
    gather x8 -> x0, local copies, waits for them, and re-layouts: 12.5 us -> none  [the longest x6 6.22 us: assemble(): jnp.take(faces3[other], jnp.clip(columns[face], 0, width - 1), axis=1)]
    dot_general x11 -> x0, matrix products: 6.96 us -> none  [the longest x6 4.11 us: assemble(): return jnp.dot(select, jnp.concatenate(pieces, 0), precision=HIGH)]
  transfers between devices with their start and end apart: 3 -> 0, of which waited for: 2 -> 0; matrix products, arithmetic and copies ran while one was open for 3% -> 0% of each run, Pallas kernels for 0% -> 0%
where the time goes in v1:
time: 57.9 us; the launch traced here: 57.3 us
  Pallas kernels  43.7 us (75%)
  local copies, waits for them, and re-layouts  12.9 us (22%)
  between operations  0.68 us (1%)
    pallas_call x1, Pallas kernels, per_device(): pl.pallas_call(functools.partial(kernel, nz, ny, nseg), out_shape=(jax.Sh...  43.7 us
    unnamed x34, local copies, waits for them, and re-layouts  12.9 us

profile of v1, /device:TPU:1, one launch (start us, length us, event | category | flops | bytes accessed | tf_op | source)
XLA Modules:
  0.0 57.3 jit_solution(9078140979853747528)
XLA Ops:
  0.6 0.0 copy-start.14
  0.6 0.0 copy-start.13
  0.7 0.0 copy-start.12
  0.7 0.7 %copy-done.14 = f32[512]{0:T(512)S(1)} copy-done((f32[512]{0:T(512)S(1)}, f32[512]{0:T(512)}, u32[]{:S(2)}) %copy-start.14) | copy-done | bytes 2072
  1.3 0.0 copy-done.13
  1.3 0.0 copy-done.12
  1.3 0.0 copy-start
  1.4 1.0 %copy-done = bf16[288,576]{1,0:T(8,128)(2,1)S(1)} copy-done((bf16[288,576]{1,0:T(8,128)(2,1)S(1)}, bf16[288,576]{1,0:T(8,128)(2,1)}, u32[]{:S(2)}) %copy-start) | copy-done | bytes 331800
  2.3 0.0 copy-start.1
  2.3 0.9 %copy-done.1 = f32[81,512]{1,0:T(8,128)S(1)} copy-done((f32[81,512]{1,0:T(8,128)S(1)}, f32[81,512]{1,0:T(8,128)}, u32[]{:S(2)}) %copy-start.1) | copy-done | bytes 165912
  3.3 0.9 %copy-done.2 = f32[81,512]{1,0:T(8,128)S(1)} copy-done((f32[81,512]{1,0:T(8,128)S(1)}, f32[81,512]{1,0:T(8,128)}, u32[]{:S(2)}) %copy-start.2) | copy-done | bytes 165912
  4.2 0.9 %copy-done.3 = f32[81,512]{1,0:T(8,128)S(1)} copy-done((f32[81,512]{1,0:T(8,128)S(1)}, f32[81,512]{1,0:T(8,128)}, u32[]{:S(2)}) %copy-start.3) | copy-done | bytes 165912
  5.1 0.9 %copy-done.4 = f32[81,512]{1,0:T(8,128)S(1)} copy-done((f32[81,512]{1,0:T(8,128)S(1)}, f32[81,512]{1,0:T(8,128)}, u32[]{:S(2)}) %copy-start.4) | copy-done | bytes 165912
  6.0 0.9 %copy-done.5 = bf16[192,256]{1,0:T(8,128)(2,1)S(1)} copy-done((bf16[192,256]{1,0:T(8,128)(2,1)S(1)}, bf16[192,256]{1,0:T(8,128)(2,1)}, u32[]{:S(2)}) %copy-start.5) | copy-done | bytes 98328
  6.9 0.9 %copy-done.6 = bf16[96,384]{1,0:T(8,128)(2,1)S(1)} copy-done((bf16[96,384]{1,0:T(8,128)(2,1)S(1)}, bf16[96,384]{1,0:T(8,128)(2,1)}, u32[]{:S(2)}) %copy-start.6) | copy-done | bytes 73752
  7.8 0.8 %copy-done.7 = f32[27,512]{1,0:T(8,128)S(1)} copy-done((f32[27,512]{1,0:T(8,128)S(1)}, f32[27,512]{1,0:T(8,128)}, u32[]{:S(2)}) %copy-start.7) | copy-done | bytes 55320
  8.6 0.8 %copy-done.8 = f32[4,32,128]{2,1,0:T(8,128)S(1)} copy-done((f32[4,32,128]{2,1,0:T(8,128)S(1)}, f32[4,32,128]{2,1,0:T(8,128)}, u32[]{:S(2)}) %copy-start.8) | copy-done | bytes 65560
  9.5 0.7 %copy-done.9 = s32[6,512]{1,0:T(8,128)S(1)} copy-done((s32[6,512]{1,0:T(8,128)S(1)}, s32[6,512]{1,0:T(8,128)}, u32[]{:S(2)}) %copy-start.9) | copy-done | bytes 12312
  10.2 0.7 %copy-done.10 = s32[6,512]{1,0:T(8,128)S(1)} copy-done((s32[6,512]{1,0:T(8,128)S(1)}, s32[6,512]{1,0:T(8,128)}, u32[]{:S(2)}) %copy-start.10) | copy-done | bytes 12312
  10.9 0.7 %copy-done.11 = f32[4,512]{1,0:T(4,128)S(1)} copy-done((f32[4,512]{1,0:T(4,128)S(1)}, f32[4,512]{1,0:T(4,128)}, u32[]{:S(2)}) %copy-start.11) | copy-done | bytes 8216
  11.6 0.7 %copy-done.15 = s32[512]{0:T(512)S(1)} copy-done((s32[512]{0:T(512)S(1)}, s32[512]{0:T(512)}, u32[]{:S(2)}) %copy-start.15) | copy-done | bytes 2072
  12.3 43.7 %shard_map.167 = (f32[81,512]{1,0:T(8,128)S(1)}, f32[4,128]{1,0:T(4,128)S(1)}) custom-call(f32[81,512]{1,0:T(8,128)S(1)} %copy-done.1, f32[81,512]{1,0:T(8,128)S(1)} %copy-done.2, f32[81,512]{1,0:T(8,128)S(1)} %copy-done.3, f32[81,512]{1,0:T(8,128)S(1)} %copy-done.4, f32[4,512]{1,0:T(4,128)S(1)} %copy-done.11, f32[27,512]{1,0:T(8,128)S(1)} %copy-done.7, ...), custom_call_target="tpu_custom_call" | custom-call | tf_op jit(solution)/shard_map/pallas_call | solution.py:333
  56.0 0.7 %copy.20 = f32[81,512]{1,0:T(8,128)} copy(f32[81,512]{1,0:T(8,128)S(1)} %get-tuple-element.8) | data formatting | bytes 331776
  56.7 0.6 %copy.21 = f32[512]{0:T(512)} copy(f32[512]{0:T(512)S(1)} %bitcast.9) | data formatting | bytes 4096
  (11 shorter events, 0.0 us)
Async XLA Ops:
  0.6 0.7 %copy-start.14 = (f32[512]{0:T(512)S(1)}, f32[512]{0:T(512)}, u32[]{:S(2)}) copy-start(f32[512]{0:T(512)} %param.24) | copy-start | bytes 6148
  0.6 0.7 %copy-start.13 = (f32[512]{0:T(512)S(1)}, f32[512]{0:T(512)}, u32[]{:S(2)}) copy-start(f32[512]{0:T(512)} %param.23) | copy-start | bytes 6148
  0.7 0.7 %copy-start.12 = (f32[512]{0:T(512)S(1)}, f32[512]{0:T(512)}, u32[]{:S(2)}) copy-start(f32[512]{0:T(512)} %param.22) | copy-start | bytes 6148
  1.3 1.0 %copy-start = (bf16[288,576]{1,0:T(8,128)(2,1)S(1)}, bf16[288,576]{1,0:T(8,128)(2,1)}, u32[]{:S(2)}) copy-start(bf16[288,576]{1,0:T(8,128)(2,1)} %constant.9.clone.force_h) | copy-start | bytes 995332
  2.3 0.9 %copy-start.1 = (f32[81,512]{1,0:T(8,128)S(1)}, f32[81,512]{1,0:T(8,128)}, u32[]{:S(2)}) copy-start(f32[81,512]{1,0:T(8,128)} %vel_f.1) | copy-start | bytes 497668
  3.3 0.9 %copy-start.2 = (f32[81,512]{1,0:T(8,128)S(1)}, f32[81,512]{1,0:T(8,128)}, u32[]{:S(2)}) copy-start(f32[81,512]{1,0:T(8,128)} %vel_i.1) | copy-start | bytes 497668
  4.2 0.9 %copy-start.3 = (f32[81,512]{1,0:T(8,128)S(1)}, f32[81,512]{1,0:T(8,128)}, u32[]{:S(2)}) copy-start(f32[81,512]{1,0:T(8,128)} %vel_a.1) | copy-start | bytes 497668
  5.1 0.9 %copy-start.4 = (f32[81,512]{1,0:T(8,128)S(1)}, f32[81,512]{1,0:T(8,128)}, u32[]{:S(2)}) copy-start(f32[81,512]{1,0:T(8,128)} %vel_ia.1) | copy-start | bytes 497668
  6.0 0.9 %copy-start.5 = (bf16[192,256]{1,0:T(8,128)(2,1)S(1)}, bf16[192,256]{1,0:T(8,128)(2,1)}, u32[]{:S(2)}) copy-start(bf16[192,256]{1,0:T(8,128)(2,1)} %constant.8.clone.rate_h) | copy-start | bytes 294916
  6.9 0.9 %copy-start.6 = (bf16[96,384]{1,0:T(8,128)(2,1)S(1)}, bf16[96,384]{1,0:T(8,128)(2,1)}, u32[]{:S(2)}) copy-start(bf16[96,384]{1,0:T(8,128)(2,1)} %constant.10.clone.place_h) | copy-start | bytes 221188
  7.8 0.8 %copy-start.7 = (f32[27,512]{1,0:T(8,128)S(1)}, f32[27,512]{1,0:T(8,128)}, u32[]{:S(2)}) copy-start(f32[27,512]{1,0:T(8,128)} %visc_h.1) | copy-start | bytes 165892
  8.6 0.8 %copy-start.8 = (f32[4,32,128]{2,1,0:T(8,128)S(1)}, f32[4,32,128]{2,1,0:T(8,128)}, u32[]{:S(2)}) copy-start(f32[4,32,128]{2,1,0:T(8,128)} %constant.11.clone.points_h) | copy-start | bytes 196612
  9.5 0.7 %copy-start.9 = (s32[6,512]{1,0:T(8,128)S(1)}, s32[6,512]{1,0:T(8,128)}, u32[]{:S(2)}) copy-start(s32[6,512]{1,0:T(8,128)} %adj_h.1) | copy-start | bytes 36868
  10.2 0.7 %copy-start.10 = (s32[6,512]{1,0:T(8,128)S(1)}, s32[6,512]{1,0:T(8,128)}, u32[]{:S(2)}) copy-start(s32[6,512]{1,0:T(8,128)} %hang_h.1) | copy-start | bytes 36868
  10.9 0.7 %copy-start.11 = (f32[4,512]{1,0:T(4,128)S(1)}, f32[4,512]{1,0:T(4,128)}, u32[]{:S(2)}) copy-start(f32[4,512]{1,0:T(4,128)} %press_h.1) | copy-start | bytes 24580
  11.6 0.7 %copy-start.15 = (s32[512]{0:T(512)S(1)}, s32[512]{0:T(512)}, u32[]{:S(2)}) copy-start(s32[512]{0:T(512)} %param.27) | copy-start | bytes 6148

commit v2 on v1

--- a/solution.py
+++ b/solution.py
@@ -81,15 +81,19 @@
     return lax.broadcasted_iota(jnp.int32, shape, dim)
 
 
+def far_first(count, stride):
+    return sorted(range(1, count), key=lambda k: -min(k // stride, (count - k) // stride))
+
+
 def kernel(
     nz, ny, nseg,
     vel_f, vel_i, vel_a, vel_ia, press_h, visc_h, scale_h, log_h, dir_h, adj_h, hang_h, own_h,
     rate_h, force_h, place_h, points_h,
-    res_out, hess_out,
+    res, hess,
     vel, press, visc, scale, log_v, dir_v, adj, hang, own, rate, force, place, points,
     rates, vstack, keys, table, side, onehot, sums, reply, gathered, partial, faces, halo, hits,
-    stress, local, spread, picked, res, hess,
-    load_sem, out_sem, key_send, key_recv, tab_send, tab_recv, side_send, side_recv,
+    stress, local, spread, picked,
+    load_sem, key_send, key_recv, tab_send, tab_recv, side_send, side_recv,
     sum_send, sum_recv, rep_send, rep_recv, par_send, par_recv, halo_send, halo_recv,
 ):
     seg, blk = lax.axis_index("seg"), lax.axis_index("blk")
@@ -113,7 +117,11 @@
         load.start()
 
     barrier = pltpu.get_barrier_semaphore()
-    peers = z_peer[1:] + y_peer[1:] + [after, before] + s_peer[1:]
+    near_s = [k for k in range(1, nseg) if k in (1, 2, 3, nseg - 3, nseg - 2, nseg - 1)]
+    near_y = [k for k in range(1, ny) if k in (1, ny - 1)]
+    peers = [y_peer[k] for k in near_y] + [s_peer[k] for k in near_s] + z_peer[1:]
+    peers += [y_peer[k] for k in range(1, ny) if k not in near_y] + [after, before]
+    peers += [s_peer[k] for k in range(1, nseg) if k not in near_s]
     for peer in peers:
         pl.semaphore_signal(barrier, inc=1, device_id=peer, device_id_type=MESH)
 
@@ -172,7 +180,7 @@
 
     pl.semaphore_wait(barrier, len(peers))
     for k in range(1, nz):
-        send(keys.at[0], keys.at[k], key_send, key_recv, z_peer[k])
+        send(keys.at[0], keys.at[k], key_send, key_recv.at[k], z_peer[k])
     for k in range(1, ny):
         send(table.at[0], table.at[k], tab_send, tab_recv, y_peer[k])
     send(table.at[0], side.at[0], side_send.at[0], side_recv.at[0], after)
@@ -187,12 +195,13 @@
         weight = jnp.where(reach != 0, jnp.where(hang[f : f + 1, :] == 1, 0.25, 1.0), 0.0)
         hits[f] = jnp.where(iota((256, 512), 0) == target, weight, 0.0).astype(BF16)
 
-    drain(keys.at[pl.ds(0, nz - 1)], key_recv)
     rho = iota((8 * ny, 512), 0)
     wanted = (z * (4 * ny) + (rho // 8) * 4 + lax.rem(rho, 4)).astype(F32)
     is_second = lax.rem(rho, 8) >= 4
     acc = jnp.zeros((16 * ny, 128), F32)
-    for d in range(nz):
+    for d in [0] + list(range(nz - 1, 0, -1)):
+        if d > 0:
+            drain(keys.at[d], key_recv.at[d])
         hit = keys[d, 0:1, :] == wanted
         value = jnp.where(is_second, keys[d, 3:4, :], keys[d, 2:3, :])
         value = jnp.where(hit, value, 0.0)
@@ -204,7 +213,7 @@
     dense = acc[0 : 8 * ny, :] + acc[8 * ny : 16 * ny, :]
     for k in range(ny):
         sums[0, k] = dense[8 * k : 8 * k + 8, :]
-    for k in range(1, ny):
+    for k in far_first(ny, 1):
         send(sums.at[0, k], sums.at[1, k], sum_send, sum_recv, y_peer[ny - k])
 
     drain(table.at[pl.ds(0, ny - 1)], tab_recv)
@@ -230,7 +239,7 @@
         mine += sums[1, k]
     share = jnp.exp(table[0, 0:4, :]) * (mine[0:4, :] + table[0, 4:8, :] * mine[4:8, :])
     partial[seg] = share
-    for k in range(1, nseg):
+    for k in far_first(nseg, 2):
         send(partial.at[seg], partial.at[seg], par_send, par_recv, s_peer[k])
 
     drain(gathered.at[pl.ds(0, nz - 1)], rep_recv)
@@ -286,8 +295,6 @@
     window(3)
     added = jnp.dot(place[...], picked[...], preferred_element_type=F32)
     res[...] = local[0:81, :] + added[0:81, :]
-    out_res = pltpu.make_async_copy(res, res_out, out_sem.at[0])
-    out_res.start()
 
     drain(side.at[0], side_recv.at[0])
     drain(side.at[1], side_recv.at[1])
@@ -305,14 +312,6 @@
     following = jnp.where(lane == 127, jnp.where(row == 7, down_side, down_row), down)
     smooth = BETA_REG * (2.0 * tile - prev - following)
 
-    drain(partial.at[pl.ds(0, nseg - 1)], par_recv)
-    result = partial[0]
-    for k in range(1, nseg):
-        result += partial[k]
-    hess[...] = result + smooth[4:8, :]
-    out_hess = pltpu.make_async_copy(hess, hess_out, out_sem.at[1])
-    out_hess.start()
-
     drain(keys.at[pl.ds(0, nz - 1)], key_send)
     drain(table.at[pl.ds(0, ny - 1)], tab_send)
     drain(sums.at[1, pl.ds(0, ny - 1)], sum_send)
@@ -321,8 +320,12 @@
     for i in range(2):
         drain(side.at[i], side_send.at[i])
         drain(halo.at[i], halo_send.at[i])
-    out_res.wait()
-    out_hess.wait()
+
+    drain(partial.at[pl.ds(0, nseg - 1)], par_recv)
+    result = partial[0]
+    for k in range(1, nseg):
+        result += partial[k]
+    hess[...] = result + smooth[4:8, :]
 
 
 def per_device(nz, ny, nseg, tables, *args):
@@ -332,9 +335,9 @@
     vmem = pltpu.VMEM
     residual, hessian = pl.pallas_call(
         functools.partial(kernel, nz, ny, nseg),
-        out_shape=(jax.ShapeDtypeStruct((81, 512), F32), jax.ShapeDtypeStruct((4, 128), F32)),
-        in_specs=[pl.BlockSpec(memory_space=pl.ANY)] * 16,
-        out_specs=(pl.BlockSpec(memory_space=pl.ANY),) * 2,
+        out_shape=(pltpu.VMEM((81, 512), F32), pltpu.VMEM((4, 128), F32)),
+        in_specs=[pl.BlockSpec(memory_space=pltpu.HBM)] * 16,
+        out_specs=(pl.BlockSpec(memory_space=pltpu.VMEM),) * 2,
         scratch_shapes=[
             vmem((4, 81, 512), F32), vmem((4, 512), F32), vmem((27, 512), F32), vmem((1, 512), F32),
             vmem((4, 128), F32), vmem((4, 128), F32), vmem((6, 512), jnp.int32), vmem((6, 512), jnp.int32),
@@ -357,16 +360,18 @@
             vmem((288, 512), F32),
             vmem((2, 8 * ny, 128), BF16),
             vmem((384, 512), BF16),
-            vmem((81, 512), F32), vmem((4, 128), F32),
-            dma((16,)), dma((2,)), dma, dma, dma, dma, dma((2,)), dma((2,)),
+            dma((16,)), dma, dma((nz,)), dma, dma, dma((2,)), dma((2,)),
             dma, dma, dma, dma, dma, dma, dma((2,)), dma((2,)),
         ],
         compiler_params=pltpu.CompilerParams(
             collective_id=0, has_side_effects=True, vmem_limit_bytes=32 * 1024 * 1024
         ),
     )(
-        *vel, press, visc, scale.reshape(1, 512), log_visc.reshape(4, 128), direction.reshape(4, 128), adj, hang,
-        owner.reshape(1, 512), *tables,
+        *[
+            pltpu.with_memory_space_constraint(x, pltpu.HBM)
+            for x in (*vel, press, visc, scale.reshape(1, 512), log_visc.reshape(4, 128), direction.reshape(4, 128), adj,
+                      hang, owner.reshape(1, 512), *tables)
+        ],
     )
     return residual, hessian.reshape(512)
 

time: 57.9 us -> 43.7 us (0.75)
  local copies, waits for them, and re-layouts: 12.9 us -> 1.25 us
  Pallas kernels: 43.7 us -> 41.6 us
    unnamed x34 -> x2, local copies, waits for them, and re-layouts: 12.9 us -> 1.25 us
    pallas_call x1, Pallas kernels: 43.7 us -> 41.6 us  [per_device(): pl.pallas_call(functools.partial(kernel, nz, ny, nseg), out_shape=(pltpu....]
where the time goes in v2:
time: 43.7 us; the launch traced here: 43.5 us
  Pallas kernels  41.6 us (95%)
  local copies, waits for them, and re-layouts  1.25 us (3%)
  between operations  0.64 us (1%)
    pallas_call x1, Pallas kernels, per_device(): pl.pallas_call(functools.partial(kernel, nz, ny, nseg), out_shape=(pltpu....  41.6 us
    unnamed x2, local copies, waits for them, and re-layouts  1.25 us

profile of v2, /device:TPU:1, one launch (start us, length us, event | category | flops | bytes accessed | tf_op | source)
XLA Modules:
  0.0 43.5 jit_solution(17931833725326149878)
XLA Ops:
  0.6 41.6 %shard_map.167 = (f32[81,512]{1,0:T(8,128)S(1)}, f32[4,128]{1,0:T(4,128)S(1)}) custom-call(f32[81,512]{1,0:T(8,128)} %vel_f.1, f32[81,512]{1,0:T(8,128)} %vel_i.1, f32[81,512]{1,0:T(8,128)} %vel_a.1, f32[81,512]{1,0:T(8,128)} %vel_ia.1, f32[4,512]{1,0:T(4,128)} %press_h.1, f32[27,512]{1,0:T(8,128)} %visc_h.1, f32[1,512]{1,0:T(1,128)} %bitcast.6, ...), custom_call_target="tpu_custom_call" | custom-call | tf_op jit(solution)/shard_map/pallas_call | solution.py:336
  42.2 0.7 %copy.20 = f32[81,512]{1,0:T(8,128)} copy(f32[81,512]{1,0:T(8,128)S(1)} %get-tuple-element.6) | data formatting | bytes 331776
  42.9 0.6 %copy.21 = f32[512]{0:T(512)} copy(f32[512]{0:T(512)S(1)} %bitcast.5) | data formatting | bytes 4096

commit v3 on v2

--- a/solution.py
+++ b/solution.py
@@ -69,7 +69,9 @@
     points[0, :27] = quad_weight[:, None]
     for d in range(3):
         points[d + 1, :27] = coords[:, d, None]
-    return rate, force, place, points
+    choose = np.zeros((192, 96), ml_dtypes.bfloat16)
+    choose[:, :81] = select.reshape(81, 192).T
+    return rate, force, place, points, choose
 
 
 def split(x):
@@ -88,10 +90,10 @@
 def kernel(
     nz, ny, nseg,
     vel_f, vel_i, vel_a, vel_ia, press_h, visc_h, scale_h, log_h, dir_h, adj_h, hang_h, own_h,
-    rate_h, force_h, place_h, points_h,
+    rate_h, force_h, place_h, points_h, choose_h,
     res, hess,
-    vel, press, visc, scale, log_v, dir_v, adj, hang, own, rate, force, place, points,
-    rates, vstack, keys, table, side, onehot, sums, reply, gathered, partial, faces, halo, hits,
+    vel, press, visc, scale, log_v, dir_v, adj, hang, own, rate, force, place, points, choose,
+    rates, vstack, keys, table, side, onehot, sums, reply, gathered, partial, packed, halo, hits,
     stress, local, spread, picked,
     load_sem, key_send, key_recv, tab_send, tab_recv, side_send, side_recv,
     sum_send, sum_recv, rep_send, rep_recv, par_send, par_recv, halo_send, halo_recv,
@@ -110,20 +112,20 @@
     pairs = [
         (vel_f, vel.at[0]), (vel_i, vel.at[1]), (vel_a, vel.at[2]), (vel_ia, vel.at[3]), (rate_h, rate), (visc_h, visc),
         (scale_h, scale), (own_h, own), (points_h, points), (log_h, log_v), (dir_h, dir_v), (adj_h, adj), (hang_h, hang),
-        (force_h, force), (press_h, press), (place_h, place),
+        (force_h, force), (press_h, press), (place_h, place), (choose_h, choose),
     ]
     loads = [pltpu.make_async_copy(a, b, load_sem.at[i]) for i, (a, b) in enumerate(pairs)]
-    for load in loads:
+    for load in loads[:5]:
         load.start()
 
     barrier = pltpu.get_barrier_semaphore()
-    near_s = [k for k in range(1, nseg) if k in (1, 2, 3, nseg - 3, nseg - 2, nseg - 1)]
-    near_y = [k for k in range(1, ny) if k in (1, ny - 1)]
-    peers = [y_peer[k] for k in near_y] + [s_peer[k] for k in near_s] + z_peer[1:]
-    peers += [y_peer[k] for k in range(1, ny) if k not in near_y] + [after, before]
-    peers += [s_peer[k] for k in range(1, nseg) if k not in near_s]
+    peers = [z_peer[k] for k in far_first(nz, 1)] + [s_peer[k] for k in far_first(nseg, 2)]
+    peers += [y_peer[k] for k in far_first(ny, 1)] + [after, before]
     for peer in peers:
         pl.semaphore_signal(barrier, inc=1, device_id=peer, device_id_type=MESH)
+
+    for load in loads[5:11]:
+        load.start()
 
     def send(src, dst, send_sem, recv_sem, peer):
         pltpu.make_async_remote_copy(
@@ -142,11 +144,11 @@
         last_low = vel[i, 80:81, :] - last_high
         row = iota((16, 512), 0)
         tail = jnp.where((row == 0) | (row == 2), last_high, jnp.where(row == 1, last_low, 0.0)).astype(BF16)
-        vstack[0:80, :] = high
-        vstack[80:160, :] = low
-        vstack[160:240, :] = high
-        vstack[240:256, :] = tail
-        rates[i] = jnp.dot(rate[...], vstack[...], preferred_element_type=F32)
+        vstack[i, 0:80, :] = high
+        vstack[i, 80:160, :] = low
+        vstack[i, 160:240, :] = high
+        vstack[i, 240:256, :] = tail
+        rates[i] = jnp.dot(rate[...], vstack[i], preferred_element_type=F32)
 
     for i in range(5, 9):
         loads[i].wait()
@@ -186,6 +188,8 @@
     send(table.at[0], side.at[0], side_send.at[0], side_recv.at[0], after)
     send(table.at[0], side.at[1], side_send.at[1], side_recv.at[1], before)
 
+    for load in loads[11:]:
+        load.start()
     loads[11].wait()
     loads[12].wait()
     lane = lax.rem(iota((1, 512), 1), 128)
@@ -217,27 +221,27 @@
         send(sums.at[0, k], sums.at[1, k], sum_send, sum_recv, y_peer[ny - k])
 
     drain(table.at[pl.ds(0, ny - 1)], tab_recv)
-    row = iota((8 * ny, 512), 0)
-    for part in range(2):
-        rows = jnp.concatenate([table[k, 4 * part : 4 * part + 4, :] for k in range(ny)], 0)
-        high, low = split(rows)
-        spread[part] = jnp.concatenate([high, low], 0)
-    key_row = z * (4 * ny) + lax.rem(iota((8 * ny, 512), 0), 4 * ny)
-    for d in range(nz):
-        pick = jnp.where(keys[d, 0:1, :] == key_row.astype(F32), 1.0, 0.0).astype(BF16)
+    rows = [
+        jnp.concatenate([table[k, 4 * part : 4 * part + 4, :] for k in range(ny)], 0) for part in range(2)
+    ]
+    high, low = split(jnp.concatenate(rows, 1).T)
+    spread[...] = jnp.concatenate([high, low], 1)
+    key_row = (z * (4 * ny) + lax.rem(iota((8 * ny, 512), 0), 4 * ny)).astype(F32)
+    for d in far_first(nz, 1) + [0]:
+        pick = jnp.where(keys[d, 0:1, :] == key_row, 1.0, 0.0).astype(BF16)
         mask = onehot[d].astype(F32)
-        for part in range(2):
-            found = lax.dot_general(spread[part], pick, (((0,), (0,)), ((), ())), preferred_element_type=F32)
-            answer = jnp.sum(found * mask, axis=0, keepdims=True)
-            reply[d, part : part + 1, :] = answer
-    for d in range(1, nz):
-        send(reply.at[d], gathered.at[d], rep_send, rep_recv, z_peer[nz - d])
-
+        found = jnp.dot(spread[...], pick, preferred_element_type=F32)
+        reply[d, 0:1, :] = jnp.sum(found[0:128] * mask, axis=0, keepdims=True)
+        reply[d, 1:2, :] = jnp.sum(found[128:256] * mask, axis=0, keepdims=True)
+        if d > 0:
+            send(reply.at[d], gathered.at[d], rep_send, rep_recv, z_peer[nz - d])
+
+    owned = jnp.exp(table[0, 0:4, :])
     drain(sums.at[1, pl.ds(0, ny - 1)], sum_recv)
     mine = sums[0, 0]
     for k in range(1, ny):
         mine += sums[1, k]
-    share = jnp.exp(table[0, 0:4, :]) * (mine[0:4, :] + table[0, 4:8, :] * mine[4:8, :])
+    share = owned * (mine[0:4, :] + table[0, 4:8, :] * mine[4:8, :])
     partial[seg] = share
     for k in far_first(nseg, 2):
         send(partial.at[seg], partial.at[seg], par_send, par_recv, s_peer[k])
@@ -248,34 +252,53 @@
         found += gathered[k]
     viscosity = jnp.exp(found[0:1, :]) * base
     direction = found[1:2, :]
-    for i in range(13, 16):
+    for i in range(13, 17):
         loads[i].wait()
     pressure = (
         press[0:1, :] + points[1][:, 0:1] * press[1:2, :] + points[2][:, 0:1] * press[2:3, :]
         + points[3][:, 0:1] * press[3:4, :]
     ) * points[0][:, 0:1] * (inverse * inverse)
-    for c in range(6):
-        at = pl.ds(32 * c, 32)
-        value = SHEAR[c] * viscosity * (rates[3, at, :] + direction * rates[2, at, :])
-        if c < 3:
-            value -= pressure
-        high, low = split(value)
-        stress[32 * c : 32 * c + 32, :] = high
-        stress[192 + 32 * c : 224 + 32 * c, :] = low
-        stress[384 + 32 * c : 416 + 32 * c, :] = high
-    local[...] = jnp.dot(force[...], stress[...], preferred_element_type=F32)
-    for b in range(4):
-        faces[b] = local[88:280, 128 * b : 128 * b + 128]
-    send(faces.at[3], halo.at[0], halo_send.at[0], halo_recv.at[0], after)
-    send(faces.at[0], halo.at[1], halo_send.at[1], halo_recv.at[1], before)
+    low_lane = iota((48, 128), 1) < 64
+    for columns in (slice(384, 512), slice(0, 128), slice(128, 384)):
+        for c in range(6):
+            at = pl.ds(32 * c, 32)
+            value = SHEAR[c] * viscosity[:, columns] * (
+                rates[3, at, columns] + direction[:, columns] * rates[2, at, columns]
+            )
+            if c < 3:
+                value -= pressure[:, columns]
+            high, low = split(value)
+            stress[32 * c : 32 * c + 32, columns] = high
+            stress[192 + 32 * c : 224 + 32 * c, columns] = low
+            stress[384 + 32 * c : 416 + 32 * c, columns] = high
+        local[:, columns] = jnp.dot(force[...], stress[:, columns], preferred_element_type=F32)
+        if columns.start == 384:
+            packed[0] = jnp.where(low_lane, pltpu.roll(local[0:48, columns], 64, 1), local[48:96, columns])
+            send(packed.at[0], halo.at[0], halo_send.at[0], halo_recv.at[0], after)
+        if columns.start == 0:
+            packed[1] = jnp.where(low_lane, local[0:48, columns], pltpu.roll(local[48:96, columns], 64, 1))
+            send(packed.at[1], halo.at[1], halo_send.at[1], halo_recv.at[1], before)
 
     low_lane = iota((192, 128), 1) < 64
 
+    def halo_faces(rows):
+        high, low = split(jnp.concatenate(rows, 0))
+        return [jnp.dot(choose[...], part, preferred_element_type=F32) for part in (high, low)]
+
+    def own_faces(b):
+        return [part.astype(F32) for part in split(local[88:280, 128 * b : 128 * b + 128])]
+
     def window(b):
-        last = halo[0] if b == 0 else faces[b - 1]
-        following = halo[1] if b == 3 else faces[b + 1]
-        beside_high, beside_low = split(jnp.where(low_lane, following, last))
-        own_high, own_low = split(faces[b])
+        if b == 0:
+            last = halo_faces([pltpu.roll(halo[0], 64, 1), halo[0]])
+        else:
+            last = own_faces(b - 1)
+        if b == 3:
+            following = halo_faces([halo[1], pltpu.roll(halo[1], 64, 1)])
+        else:
+            following = own_faces(b + 1)
+        beside_high, beside_low = [jnp.where(low_lane, n, p).astype(BF16) for n, p in zip(following, last)]
+        own_high, own_low = split(local[88:280, 128 * b : 128 * b + 128])
         for f in range(6):
             at = slice(32 * f, 32 * f + 32)
             window_rows = jnp.concatenate([
@@ -287,14 +310,16 @@
             picked[32 * other : 32 * other + 32, 128 * b : 128 * b + 128] = got[0:32].astype(BF16)
             picked[192 + 32 * other : 224 + 32 * other, 128 * b : 128 * b + 128] = got[32:64].astype(BF16)
 
+    def settle(columns):
+        added = jnp.dot(place[...], picked[:, columns], preferred_element_type=F32)
+        res[:, columns] = local[0:81, columns] + added[0:81, :]
+
     window(1)
     window(2)
-    drain(halo.at[0], halo_recv.at[0])
-    window(0)
+    settle(slice(128, 384))
     drain(halo.at[1], halo_recv.at[1])
     window(3)
-    added = jnp.dot(place[...], picked[...], preferred_element_type=F32)
-    res[...] = local[0:81, :] + added[0:81, :]
+    settle(slice(384, 512))
 
     drain(side.at[0], side_recv.at[0])
     drain(side.at[1], side_recv.at[1])
@@ -321,11 +346,26 @@
         drain(side.at[i], side_send.at[i])
         drain(halo.at[i], halo_send.at[i])
 
+    drain(halo.at[0], halo_recv.at[0])
+    window(0)
+    settle(slice(0, 128))
+
     drain(partial.at[pl.ds(0, nseg - 1)], par_recv)
     result = partial[0]
     for k in range(1, nseg):
         result += partial[k]
     hess[...] = result + smooth[4:8, :]
+
+
+def deliver(res_in, hess_in, res_out, hess_out, sem):
+    copies = [
+        pltpu.make_async_copy(res_in, res_out, sem.at[0]),
+        pltpu.make_async_copy(hess_in, hess_out, sem.at[1]),
+    ]
+    for copy in copies:
+        copy.start()
+    for copy in copies:
+        copy.wait()
 
 
 def per_device(nz, ny, nseg, tables, *args):
@@ -336,15 +376,15 @@
     residual, hessian = pl.pallas_call(
         functools.partial(kernel, nz, ny, nseg),
         out_shape=(pltpu.VMEM((81, 512), F32), pltpu.VMEM((4, 128), F32)),
-        in_specs=[pl.BlockSpec(memory_space=pltpu.HBM)] * 16,
+        in_specs=[pl.BlockSpec(memory_space=pltpu.HBM)] * 17,
         out_specs=(pl.BlockSpec(memory_space=pltpu.VMEM),) * 2,
         scratch_shapes=[
             vmem((4, 81, 512), F32), vmem((4, 512), F32), vmem((27, 512), F32), vmem((1, 512), F32),
             vmem((4, 128), F32), vmem((4, 128), F32), vmem((6, 512), jnp.int32), vmem((6, 512), jnp.int32),
             vmem((1, 512), jnp.int32),
-            vmem((192, 256), BF16), vmem((288, 576), BF16), vmem((96, 384), BF16), vmem((4, 32, 128), F32),
+            vmem((192, 256), BF16), vmem((288, 576), BF16), vmem((96, 384), BF16), vmem((4, 32, 128), F32), vmem((192, 96), BF16),
             vmem((4, 192, 512), F32),
-            vmem((256, 512), BF16),
+            vmem((4, 256, 512), BF16),
             vmem((nz, 4, 512), F32),
             vmem((ny, 8, 128), F32),
             vmem((2, 8, 128), F32),
@@ -353,14 +393,14 @@
             vmem((nz, 2, 512), F32),
             vmem((nz, 2, 512), F32),
             vmem((nseg, 4, 128), F32),
-            vmem((4, 192, 128), F32),
-            vmem((2, 192, 128), F32),
+            vmem((2, 48, 128), F32),
+            vmem((2, 48, 128), F32),
             vmem((6, 256, 512), BF16),
             vmem((576, 512), BF16),
             vmem((288, 512), F32),
-            vmem((2, 8 * ny, 128), BF16),
+            vmem((256, 8 * ny), BF16),
             vmem((384, 512), BF16),
-            dma((16,)), dma, dma((nz,)), dma, dma, dma((2,)), dma((2,)),
+            dma((17,)), dma, dma((nz,)), dma, dma, dma((2,)), dma((2,)),
             dma, dma, dma, dma, dma, dma, dma((2,)), dma((2,)),
         ],
         compiler_params=pltpu.CompilerParams(
@@ -373,6 +413,13 @@
                       hang, owner.reshape(1, 512), *tables)
         ],
     )
+    residual, hessian = pl.pallas_call(
+        deliver,
+        out_shape=(jax.ShapeDtypeStruct((81, 512), F32), jax.ShapeDtypeStruct((4, 128), F32)),
+        in_specs=[pl.BlockSpec(memory_space=pltpu.VMEM)] * 2,
+        out_specs=(pl.BlockSpec(memory_space=pl.ANY),) * 2,
+        scratch_shapes=[dma((2,))],
+    )(*[pltpu.with_memory_space_constraint(x, pltpu.VMEM) for x in (residual, hessian)])
     return residual, hessian.reshape(512)
 
 

time: 43.7 us -> 41.3 us (0.945)
  local copies, waits for them, and re-layouts: 1.25 us -> 0 us
  Pallas kernels: 41.6 us -> 40.4 us
    pallas_call x1, Pallas kernels: 41.6 us -> 39.7 us  [per_device(): pl.pallas_call(functools.partial(kernel, nz, ny, nseg), out_shape=(pltpu....]
    unnamed x2 -> x0, local copies, waits for them, and re-layouts: 1.25 us -> none
    pallas_call x0 -> x1, Pallas kernels: none -> 0.69 us  [per_device(): pl.pallas_call(deliver, out_shape=(jax.ShapeDtypeStruct((81, 512), F32),...]
where the time goes in v3:
time: 41.3 us; the launch traced here: 41 us
  Pallas kernels  40.4 us (98%)
  between operations  0.64 us (2%)
    pallas_call x1, Pallas kernels, per_device(): pl.pallas_call(functools.partial(kernel, nz, ny, nseg), out_shape=(pltpu....  39.7 us

profile of v3, /device:TPU:1, one launch (start us, length us, event | category | flops | bytes accessed | tf_op | source)
XLA Modules:
  0.0 41.0 jit_solution(10068611081290793029)
XLA Ops:
  0.6 39.7 %shard_map.176 = (f32[81,512]{1,0:T(8,128)S(1)}, f32[4,128]{1,0:T(4,128)S(1)}) custom-call(f32[81,512]{1,0:T(8,128)} %vel_f.1, f32[81,512]{1,0:T(8,128)} %vel_i.1, f32[81,512]{1,0:T(8,128)} %vel_a.1, f32[81,512]{1,0:T(8,128)} %vel_ia.1, f32[4,512]{1,0:T(4,128)} %press_h.1, f32[27,512]{1,0:T(8,128)} %visc_h.1, f32[1,512]{1,0:T(1,128)} %bitcast.5, ...), custom_call_target="tpu_custom_call" | custom-call | tf_op jit(solution)/shard_map/pallas_call | solution.py:376
  40.3 0.7 %shard_map.177 = (f32[81,512]{1,0:T(8,128)}, f32[4,128]{1,0:T(4,128)}) custom-call(f32[81,512]{1,0:T(8,128)S(1)} %get-tuple-element.6.res_in, f32[4,128]{1,0:T(4,128)S(1)} %get-tuple-element.7.hess_in), custom_call_target="tpu_custom_call" | custom-call | tf_op jit(solution)/shard_map/pallas_call | solution.py:416

commit v4 on v3

--- a/solution.py
+++ b/solution.py
@@ -119,7 +119,8 @@
         load.start()
 
     barrier = pltpu.get_barrier_semaphore()
-    peers = [z_peer[k] for k in far_first(nz, 1)] + [s_peer[k] for k in far_first(nseg, 2)]
+    far_s = far_first(nseg, 2)
+    peers = [s_peer[k] for k in far_s[:3]] + [z_peer[k] for k in far_first(nz, 1)] + [s_peer[k] for k in far_s[3:]]
     peers += [y_peer[k] for k in far_first(ny, 1)] + [after, before]
     for peer in peers:
         pl.semaphore_signal(barrier, inc=1, device_id=peer, device_id_type=MESH)
@@ -243,7 +244,8 @@
         mine += sums[1, k]
     share = owned * (mine[0:4, :] + table[0, 4:8, :] * mine[4:8, :])
     partial[seg] = share
-    for k in far_first(nseg, 2):
+    in_turn = far_first(nseg, 2)
+    for k in in_turn[:10]:
         send(partial.at[seg], partial.at[seg], par_send, par_recv, s_peer[k])
 
     drain(gathered.at[pl.ds(0, nz - 1)], rep_recv)
@@ -279,6 +281,8 @@
             packed[1] = jnp.where(low_lane, local[0:48, columns], pltpu.roll(local[48:96, columns], 64, 1))
             send(packed.at[1], halo.at[1], halo_send.at[1], halo_recv.at[1], before)
 
+    for k in in_turn[10:]:
+        send(partial.at[seg], partial.at[seg], par_send, par_recv, s_peer[k])
     low_lane = iota((192, 128), 1) < 64
 
     def halo_faces(rows):
@@ -337,6 +341,16 @@
     following = jnp.where(lane == 127, jnp.where(row == 7, down_side, down_row), down)
     smooth = BETA_REG * (2.0 * tile - prev - following)
 
+    drain(halo.at[0], halo_recv.at[0])
+    window(0)
+    settle(slice(0, 128))
+
+    drain(partial.at[pl.ds(0, nseg - 1)], par_recv)
+    result = partial[0]
+    for k in range(1, nseg):
+        result += partial[k]
+    hess[...] = result + smooth[4:8, :]
+
     drain(keys.at[pl.ds(0, nz - 1)], key_send)
     drain(table.at[pl.ds(0, ny - 1)], tab_send)
     drain(sums.at[1, pl.ds(0, ny - 1)], sum_send)
@@ -345,16 +359,6 @@
     for i in range(2):
         drain(side.at[i], side_send.at[i])
         drain(halo.at[i], halo_send.at[i])
-
-    drain(halo.at[0], halo_recv.at[0])
-    window(0)
-    settle(slice(0, 128))
-
-    drain(partial.at[pl.ds(0, nseg - 1)], par_recv)
-    result = partial[0]
-    for k in range(1, nseg):
-        result += partial[k]
-    hess[...] = result + smooth[4:8, :]
 
 
 def deliver(res_in, hess_in, res_out, hess_out, sem):

time: 41.3 us -> 41.2 us (level)
  no operation moved by 1% of the time
where the time goes in v4:
time: 41.2 us; the launch traced here: 41 us
  Pallas kernels  40.4 us (98%)
  between operations  0.64 us (2%)
    pallas_call x1, Pallas kernels, per_device(): pl.pallas_call(functools.partial(kernel, nz, ny, nseg), out_shape=(pltpu....  39.7 us

profile of v4, /device:TPU:1, one launch (start us, length us, event | category | flops | bytes accessed | tf_op | source)
XLA Modules:
  0.0 41.0 jit_solution(13323173000142286996)
XLA Ops:
  0.6 39.7 %shard_map.176 = (f32[81,512]{1,0:T(8,128)S(1)}, f32[4,128]{1,0:T(4,128)S(1)}) custom-call(f32[81,512]{1,0:T(8,128)} %vel_f.1, f32[81,512]{1,0:T(8,128)} %vel_i.1, f32[81,512]{1,0:T(8,128)} %vel_a.1, f32[81,512]{1,0:T(8,128)} %vel_ia.1, f32[4,512]{1,0:T(4,128)} %press_h.1, f32[27,512]{1,0:T(8,128)} %visc_h.1, f32[1,512]{1,0:T(1,128)} %bitcast.5, ...), custom_call_target="tpu_custom_call" | custom-call | tf_op jit(solution)/shard_map/pallas_call | solution.py:380
  40.3 0.7 %shard_map.177 = (f32[81,512]{1,0:T(8,128)}, f32[4,128]{1,0:T(4,128)}) custom-call(f32[81,512]{1,0:T(8,128)S(1)} %get-tuple-element.6.res_in, f32[4,128]{1,0:T(4,128)S(1)} %get-tuple-element.7.hess_in), custom_call_target="tpu_custom_call" | custom-call | tf_op jit(solution)/shard_map/pallas_call | solution.py:420
